TPU v7x, 128 devices: a whole 4x4x4 slice. The times are simulated.
128 devices in a mesh: node: 8 (over z, core), local: 16 (over x, y).
Axes of the slice: x: 4, y: 4, z: 4, core: 2. Of those that a mesh axis runs over, the one named last changes fastest.
Arguments:
- saved_input: bfloat16 [4096, 3584], P('local'), may hold values from -6 to 6
- out_grad: bfloat16 [4096, 3584], P('local'), may hold values from -6 to 6
- routes: int32 [4096, 2], P('local'), may hold values from 0 to 15, all different within a row; in each aligned block of 256 rows (0 to 255, 256 to 511, ...) at most 64 rows name the same one
- gates: bfloat16 [4096, 2], P('local'), may hold values from 0.049804688 to 1
- gate_weight: bfloat16 [16, 3584, 2048], P('local', None, 'node'), may hold values from -0.09375 to 0.09375
- up_weight: bfloat16 [16, 3584, 2048], P('local', None, 'node'), may hold values from -0.09375 to 0.09375
- down_weight: bfloat16 [16, 2048, 3584], P('local', 'node'), may hold values from -0.125 to 0.125
Outputs:
- grad_input: bfloat16 [4096, 3584], P('local', 'node')
- grad_gates: float32 [4096, 2], P('local')
- grad_gate_weight: float32 [16, 3584, 2048], P('local', None, 'node')
- grad_up_weight: float32 [16, 3584, 2048], P('local', None, 'node')
- grad_down_weight: float32 [16, 2048, 3584], P('local', 'node')
Inputs may be any that keep to these rules, and one draw needn't show every extreme that they name: `routes`: the 2 experts of a token differ. In each aligned block of 256 tokens (the tokens on one device along local) no expert is chosen by more than 64 tokens, and some expert is chosen by exactly 64.
All inputs are finite; a program needn't handle non-finite values.
Results may differ from a plain program's by a relative error of at most 0.0049.
Values may be sent and summed in bfloat16 or wider, within the bound.
A program may use at most 192 MiB of HBM per device.

v0:
```python
import jax
import jax.numpy as jnp
from jax import lax
from jax.sharding import PartitionSpec as P


def slot_layout(routes, experts, capacity):
    flat_ids = routes.reshape(-1)
    labels = jnp.arange(experts, dtype=jnp.int32)
    onehot = (flat_ids[:, None] == labels[None, :]).astype(jnp.int32)
    earlier = jnp.cumsum(onehot, axis=0) - onehot
    ranked = jnp.sum(earlier * onehot, axis=1)
    return flat_ids * capacity + ranked


def pick_rows(table, target, tokens_here, picks):
    picked = jnp.take(table, target, axis=0)
    return jnp.sum(picked.reshape(tokens_here, picks, table.shape[1]), axis=1)


def on_device(saved_input, out_grad, routes, gates, gate_weight, up_weight, down_weight):
    experts = lax.axis_size("local")
    tokens_here = saved_input.shape[0]
    features = saved_input.shape[1]
    picks = routes.shape[1]
    capacity = 2 * tokens_here * picks // experts
    slot_rows = experts * capacity
    hidden_here = gate_weight.shape[2]
    target = slot_layout(routes, experts, capacity)
    owner = jnp.arange(tokens_here * picks, dtype=jnp.int32) // picks
    send_input = (
        jnp.zeros((slot_rows, features), jnp.bfloat16)
        .at[target]
        .set(saved_input[owner])
        .reshape(experts, capacity, features)
    )
    send_grad = (
        jnp.zeros((slot_rows, features), jnp.bfloat16)
        .at[target]
        .set(out_grad[owner])
        .reshape(experts, capacity, features)
    )
    send_gate = (
        jnp.zeros((slot_rows,), jnp.bfloat16)
        .at[target]
        .set(gates.reshape(-1))
        .reshape(experts, capacity)
    )
    recv_input, recv_grad, recv_gate = (
        lax.all_to_all(send_input, "local", split_axis=0, concat_axis=0, tiled=True),
        lax.all_to_all(send_grad, "local", split_axis=0, concat_axis=0, tiled=True),
        lax.all_to_all(send_gate, "local", split_axis=0, concat_axis=0, tiled=True),
    )
    inputs = recv_input.reshape(slot_rows, features)
    upstream = recv_grad.reshape(slot_rows, features)
    row_gate = recv_gate.reshape(slot_rows).astype(jnp.float32)[:, None]
    gate_both = jnp.concatenate([gate_weight[0], up_weight[0]], axis=1)
    pre_both = jnp.dot(inputs, gate_both, preferred_element_type=jnp.float32)
    gate_pre = pre_both[:, :hidden_here]
    up_pre = pre_both[:, hidden_here:]
    contract_feat = (((1,), (1,)), ((), ()))
    back_proj = lax.dot_general(
        upstream, down_weight[0], contract_feat, preferred_element_type=jnp.float32
    )
    sigmoid = jax.nn.sigmoid(gate_pre)
    activated = gate_pre * sigmoid
    gate_term = jnp.sum(activated * up_pre * back_proj, axis=1)
    scaled_hidden = (row_gate * activated * up_pre).astype(jnp.bfloat16)
    hidden_grad = row_gate * back_proj
    grad_gate_pre = hidden_grad * up_pre * sigmoid * (1.0 + gate_pre * (1.0 - sigmoid))
    grad_up_pre = hidden_grad * activated
    grad_pre_both = jnp.concatenate([grad_gate_pre, grad_up_pre], axis=1).astype(jnp.bfloat16)
    contract_rows = (((0,), (0,)), ((), ()))
    grad_down = lax.dot_general(
        scaled_hidden, upstream, contract_rows, preferred_element_type=jnp.float32
    )
    grad_weights = lax.dot_general(
        inputs, grad_pre_both, contract_rows, preferred_element_type=jnp.float32
    )
    partial_value = lax.dot_general(
        grad_pre_both, gate_both, contract_feat, preferred_element_type=jnp.float32
    )
    gate_sum = lax.psum(gate_term, "node").reshape(experts, capacity)
    back_input, back_gate = (
        lax.all_to_all(
            partial_value.reshape(experts, capacity, features),
            "local",
            split_axis=0,
            concat_axis=0,
            tiled=True,
        ),
        lax.all_to_all(gate_sum, "local", split_axis=0, concat_axis=0, tiled=True),
    )
    summed = pick_rows(back_input.reshape(slot_rows, features), target, tokens_here, picks)
    grad_input = lax.psum_scatter(summed, "node", scatter_dimension=1, tiled=True).astype(
        jnp.bfloat16
    )
    grad_gates = jnp.take(back_gate.reshape(-1), target).reshape(tokens_here, picks)
    grad_gate_weight = grad_weights[:, :hidden_here][None]
    grad_up_weight = grad_weights[:, hidden_here:][None]
    grad_down_weight = grad_down[None]
    return (grad_input, grad_gates, grad_gate_weight, grad_up_weight, grad_down_weight)


def solution(mesh):
    placed = (
        P("local", None),
        P("local", None),
        P("local", None),
        P("local", None),
        P("local", None, "node"),
        P("local", None, "node"),
        P("local", "node", None),
    )
    return jax.shard_map(
        on_device,
        mesh=mesh,
        in_specs=placed,
        out_specs=(
            P("local", "node"),
            P("local", None),
            P("local", None, "node"),
            P("local", None, "node"),
            P("local", "node", None),
        ),
        check_vma=False,
    )
```

profile of v0, /device:TPU:1, one launch (start us, length us, event | category | flops | bytes accessed | tf_op | source)
XLA Modules:
  0.0 677.2 jit_solution(3178480225662959838)
XLA Ops:
  7.2 0.9 copy.27
  8.4 0.8 copy.31
  9.4 1.2 reduce-window.6
  11.1 3.8 scatter_custom_fusion
  14.9 0.7 all_to_all.28
  15.5 7.8 %all-to-all-start = ((bf16[16,1,64]{2,1,0:T(2,128)(2,1)}), bf16[16,1,64]{2,1,0:T(2,128)(2,1)S(1)}, u32[]{:S(2)}, u32[]{:S(2)}) async-start(bf16[16,1,64]{2,1,0:T(2,128)(2,1)} %all_to_all.28), calls=%async_computation | async-start | bytes 16384 | tf_op jit(solution)/shard_map/all_to_all | solution.py:52
  23.3 20.7 %scatter_custom_fusion.2 = bf16[1024,3584]{1,0:T(8,128)(2,1)} fusion(s32[512]{0:T(512)S(1)} %bitcast.57, bf16[256,3584]{1,0:T(8,128)(2,1)S(1)} %copy-done, s32[1024]{0:T(1024)S(1)} %pad_clamp_fusion.1, bf16[]{:T(256)} %constant.54.clone.1), kind=kCustom, calls=%fused_computation.12 | custom fusion | bytes 7340034 | tf_op jit(solution)/shard_map/scatter | solution.py:34
  44.1 7.1 %all-to-all-start.2 = ((bf16[16,64,3584]{2,1,0:T(8,128)(2,1)}), bf16[16,64,3584]{2,1,0:T(8,128)(2,1)}, u32[]{:S(2)}, u32[]{:S(2)}) async-start(bf16[16,64,3584]{2,1,0:T(8,128)(2,1)} %bitcast.51), calls=%async_computation.2 | async-start | bytes 14680064 | tf_op jit(solution)/shard_map/all_to_all | solution.py:50
  51.2 18.7 %scatter_custom_fusion.1 = bf16[1024,3584]{1,0:T(8,128)(2,1)} fusion(s32[512]{0:T(512)S(1)} %bitcast.58, bf16[256,3584]{1,0:T(8,128)(2,1)} %param.8, s32[1024]{0:T(1024)S(1)} %pad_clamp_fusion.1, bf16[]{:T(256)} %constant.54.clone.1), kind=kCustom, calls=%fused_computation.14 | custom fusion | bytes 7340544 | tf_op jit(solution)/shard_map/scatter | solution.py:40
  69.9 96.2 %all-to-all-done.2 = bf16[16,64,3584]{2,1,0:T(8,128)(2,1)} async-done(((bf16[16,64,3584]{2,1,0:T(8,128)(2,1)}), bf16[16,64,3584]{2,1,0:T(8,128)(2,1)}, u32[]{:S(2)}, u32[]{:S(2)}) %all-to-all-start.2) | async-done | bytes 7340064 | tf_op jit(solution)/shard_map/all_to_all | solution.py:50
  166.0 11.5 %all-to-all-start.1 = ((bf16[16,64,3584]{2,1,0:T(8,128)(2,1)}), bf16[16,64,3584]{2,1,0:T(8,128)(2,1)}, u32[]{:S(2)}, u32[]{:S(2)}) async-start(bf16[16,64,3584]{2,1,0:T(8,128)(2,1)} %bitcast.50), calls=%async_computation.1 | async-start | bytes 14680064 | tf_op jit(solution)/shard_map/all_to_all | solution.py:51
  177.7 9.4 %fusion.7 = f32[1024,512]{0,1:T(8,128)} fusion(bf16[1024,3584]{1,0:T(8,128)(2,1)} %bitcast.8, bf16[3584,256]{1,0:T(8,128)(2,1)} %bitcast.61, bf16[3584,256]{1,0:T(8,128)(2,1)} %bitcast.63), kind=kOutput, calls=%fused_computation.19 | convolution fusion | flops 3765436416 | bytes 13107200 | tf_op jit(solution)/shard_map/dot_general | solution.py:58
  187.1 91.2 %all-to-all-done.1 = bf16[16,64,3584]{2,1,0:T(8,128)(2,1)} async-done(((bf16[16,64,3584]{2,1,0:T(8,128)(2,1)}), bf16[16,64,3584]{2,1,0:T(8,128)(2,1)}, u32[]{:S(2)}, u32[]{:S(2)}) %all-to-all-start.1) | async-done | bytes 7340064 | tf_op jit(solution)/shard_map/all_to_all | solution.py:51
  278.3 6.6 multiply_convert_fusion.2
  285.0 20.4 %psum.7 = f32[16,1,64]{2,1,0:T(1,128)} all-reduce(f32[16,1,64]{2,1,0:T(1,128)S(1)} %all_to_all.26), channel_id=1, replica_groups=mesh['node'=8,'local'=16] {'node'}, use_global_device_ids=true, to_apply=%region_9.10 | all-reduce | flops 1024 | bytes 8192 | tf_op jit(solution)/shard_map/psum | solution.py:83
  305.4 7.5 %all-to-all-start.4 = ((f32[16,1,64]{2,1,0:T(1,128)}), f32[16,1,64]{2,1,0:T(1,128)S(1)}, u32[]{:S(2)}, u32[]{:S(2)}) async-start(f32[16,1,64]{2,1,0:T(1,128)} %psum.7), calls=%async_computation.4 | async-start | bytes 16384 | tf_op jit(solution)/shard_map/all_to_all | solution.py:92
  312.9 9.4 %fusion.6 = f32[1024,3584]{1,0:T(8,128)} fusion(bf16[3584,256]{1,0:T(8,128)(2,1)} %bitcast.62, bf16[3584,256]{1,0:T(8,128)(2,1)} %bitcast.64, bf16[1024,256]{0,1:T(8,128)(2,1)S(1)} %get-tuple-element.25, bf16[1024,256]{0,1:T(8,128)(2,1)S(1)} %get-tuple-element.24), kind=kOutput, calls=%fused_computation.18 | convolution fusion | flops 3767533568 | bytes 19398656 | tf_op jit(solution)/shard_map/dot_general | solution.py:80
  322.4 6.7 all-to-all-start.3
  329.8 0.7 reduce.9
  330.5 2.5 gather_fusion.1
  333.3 247.9 %all-to-all-done.3 = f32[16,64,3584]{2,1,0:T(8,128)} async-done(((f32[16,64,3584]{2,1,0:T(8,128)}), f32[16,64,3584]{2,1,0:T(8,128)}, u32[]{:S(2)}, u32[]{:S(2)}) %all-to-all-start.3) | async-done | bytes 14680096 | tf_op jit(solution)/shard_map/all_to_all | solution.py:85
  581.2 13.3 %gather_fusion = f32[512,3584]{1,0:T(8,128)} fusion(f32[1024,3584]{1,0:T(8,128)} %bitcast.12, s32[1024]{0:T(1024)S(1)} %pad_clamp_fusion), kind=kCustom, calls=%fused_computation.2 | custom fusion | bytes 14682112 | tf_op jit(solution)/shard_map/jit(_take)/gather | solution.py:17
  594.5 9.3 %gather.21 = f32[256,2,3584]{2,1,0:T(2,128)} reshape(f32[512,3584]{1,0:T(8,128)} %gather_fusion) | data formatting | bytes 14680064 | tf_op jit(solution)/shard_map/jit(_take)/gather | solution.py:17
  603.8 14.6 %select_reduce_fusion = f32[256,3584]{1,0:T(8,128)} fusion(f32[256,2,3584]{2,1,0:T(2,128)} %gather.21, pred[256,2]{1,0:T(8,128)(4,1)S(1)} %get-tuple-element.21), kind=kLoop, calls=%fused_computation.7 | loop fusion | flops 2752512 | bytes 11010560 | tf_op jit(solution)/shard_map/reduce_sum | solution.py:18
  618.4 5.1 copy.35
  623.6 7.7 %convolution_bitcast_fusion = f32[1,256,3584]{2,1,0:T(8,128)} fusion(bf16[1024,3584]{1,0:T(8,128)(2,1)} %bitcast.5, f32[1024,512]{0,1:T(8,128)} %fusion.7, f32[1024]{0:T(1024)S(1)} %reshape.170), kind=kOutput, calls=%fused_computation.8 | convolution fusion | flops 1880883200 | bytes 13111296 | tf_op jit(solution)/shard_map/dot_general | solution.py:74
  631.2 6.3 fusion.11
  637.6 3.6 slice_bitcast_fusion
  641.2 0.7 copy.34
  641.9 26.3 %reduce-scatter.4.cloned.1.call-done = f32[448,256]{1,0:T(8,128)} async-done(((f32[3584,256]{1,0:T(8,128)}), f32[448,256]{1,0:T(8,128)}) %reduce-scatter.4.cloned.1.call-update) | async-done | bytes 458768
  668.1 1.2 copy.36
  669.3 0.8 copy.33
  (30 shorter events, 2.1 us)
Async XLA Ops:
  7.2 16.2 %copy-start = (bf16[256,3584]{1,0:T(8,128)(2,1)S(1)}, bf16[256,3584]{1,0:T(8,128)(2,1)}, u32[]{:S(2)}) copy-start(bf16[256,3584]{1,0:T(8,128)(2,1)} %param.7) | copy-start | bytes 5505028
  15.5 28.6 %all-to-all-start = ((bf16[16,1,64]{2,1,0:T(2,128)(2,1)}), bf16[16,1,64]{2,1,0:T(2,128)(2,1)S(1)}, u32[]{:S(2)}, u32[]{:S(2)}) async-start(bf16[16,1,64]{2,1,0:T(2,128)(2,1)} %all_to_all.28), calls=%async_computation | async-start | bytes 16384 | tf_op jit(solution)/shard_map/all_to_all | solution.py:52
  44.1 121.9 %all-to-all-start.2 = ((bf16[16,64,3584]{2,1,0:T(8,128)(2,1)}), bf16[16,64,3584]{2,1,0:T(8,128)(2,1)}, u32[]{:S(2)}, u32[]{:S(2)}) async-start(bf16[16,64,3584]{2,1,0:T(8,128)(2,1)} %bitcast.51), calls=%async_computation.2 | async-start | bytes 14680064 | tf_op jit(solution)/shard_map/all_to_all | solution.py:50
  166.0 112.3 %all-to-all-start.1 = ((bf16[16,64,3584]{2,1,0:T(8,128)(2,1)}), bf16[16,64,3584]{2,1,0:T(8,128)(2,1)}, u32[]{:S(2)}, u32[]{:S(2)}) async-start(bf16[16,64,3584]{2,1,0:T(8,128)(2,1)} %bitcast.50), calls=%async_computation.1 | async-start | bytes 14680064 | tf_op jit(solution)/shard_map/all_to_all | solution.py:51
  305.4 16.9 %all-to-all-start.4 = ((f32[16,1,64]{2,1,0:T(1,128)}), f32[16,1,64]{2,1,0:T(1,128)S(1)}, u32[]{:S(2)}, u32[]{:S(2)}) async-start(f32[16,1,64]{2,1,0:T(1,128)} %psum.7), calls=%async_computation.4 | async-start | bytes 16384 | tf_op jit(solution)/shard_map/all_to_all | solution.py:92
  322.4 258.8 %all-to-all-start.3 = ((f32[16,64,3584]{2,1,0:T(8,128)}), f32[16,64,3584]{2,1,0:T(8,128)}, u32[]{:S(2)}, u32[]{:S(2)}) async-start(f32[16,64,3584]{2,1,0:T(8,128)} %bitcast.52), calls=%async_computation.3 | async-start | bytes 29360128 | tf_op jit(solution)/shard_map/all_to_all | solution.py:85
  329.1 339.1 %reduce-scatter.4.cloned.1.call-start = ((), (), s32[]{:S(2)}) async-start(), calls=%async_computation.6 | async-start | bytes 4128768
  637.6 32.5 %copy-start.1 = (bf16[256,3584]{1,0:T(8,128)(2,1)S(1)}, bf16[256,3584]{1,0:T(8,128)(2,1)}, u32[]{:S(2)}) copy-start(bf16[256,3584]{1,0:T(8,128)(2,1)} %param.7) | copy-start | bytes 5505028
Sparse Core Ops, SparseCore 0:
  623.7 44.3 reduce-scatter.3
where the time goes:
time: 684 us; the launch traced here: 677 us
  waiting for transfers between devices  462 us (68%)
  local copies, waits for them, and re-layouts  84 us (12%)
  starting transfers between devices  40.6 us (6%)
  matrix products  39.4 us (6%)
  blocking collectives  20.4 us (3%)
  other arithmetic  16.7 us (2%)
  between operations  14.5 us (2%)
    all_to_all x1, waiting for transfers between devices, on_device(): lax.all_to_all(partial_value.reshape(experts, capacity, features), 'local...  248 us
    all_to_all x1, waiting for transfers between devices, on_device(): lax.all_to_all(send_input, 'local', split_axis=0, concat_axis=0, tiled=True)  96.2 us
    all_to_all x1, waiting for transfers between devices, on_device(): lax.all_to_all(send_grad, 'local', split_axis=0, concat_axis=0, tiled=True)  91.2 us
    unnamed x2, waiting for transfers between devices  26.3 us
    gather x2, local copies, waits for them, and re-layouts, pick_rows(): picked = jnp.take(table, target, axis=0)  22.6 us
    scatter x1, local copies, waits for them, and re-layouts, on_device(): send_input = jnp.zeros((slot_rows, features), jnp.bfloat16).at[target].se...  20.7 us
    psum x1, blocking collectives, on_device(): gate_sum = lax.psum(gate_term, 'node').reshape(experts, capacity)  20.4 us
    scatter x1, local copies, waits for them, and re-layouts, on_device(): send_grad = jnp.zeros((slot_rows, features), jnp.bfloat16).at[target].set...  18.7 us
  transfers between devices with their start and end apart: 6, of which 4 were waited for; matrix products, arithmetic and copies ran while one was open for 12% of the time, Pallas kernels for 0%

commit v1 on v0

v1 whole, which is shorter than its diff:
```python
import functools

import jax
import jax.numpy as jnp
from jax import lax
from jax.experimental import pallas as pl
from jax.experimental.pallas import tpu as pltpu
from jax.sharding import PartitionSpec as P

MESH = pl.DeviceIdType.MESH
F32 = jnp.float32
BF16 = jnp.bfloat16
TOK = 256
FEAT = 3584
QUART = FEAT // 4
HID = 256
CAP = 64
ROWS = 16 * CAP
CHUNK = 4 * CAP
HALF = CHUNK // 2
WIN = 512
TILE = 512


def dot(a, b, dims):
    return lax.dot_general(a, b, (dims, ((), ())), preferred_element_type=F32)


def kernel(
    saved, ograd, routes, gates, gate_w, up_w, down_w,
    gin_o, gg_o, ggw_o, guw_o, gdw_o,
    tok, send, onehot, gsend, grecv, xy, w, wd, grad_pre, hidden, part,
    sib_in, z_in, ret, back, gt_send, gt_recv, gt_sib, gt_mine, gt_z,
    comb, comb_sib, opp_out, opp_in, dw_gu, dw_d,
    load_sem, disp_send, disp_recv, gate_send, gate_recv, fz_send, fz_recv, fs_send, fs_recv,
    sib_send, sib_recv, zr_send, zr_recv, ret_send, ret_recv, gts_send, gts_recv, gtx_send, gtx_recv,
    gtz_send, gtz_recv, cs_send, cs_recv, op_send, op_recv, out_sem,
):
    n, l = lax.axis_index("node"), lax.axis_index("local")
    z, c = lax.div(n, 2), lax.rem(n, 2)
    x, y = lax.div(l, 4), lax.rem(l, 4)
    other = 1 - c

    def plane(dx, dy):
        return (n, lax.rem(x + dx, 4) * 4 + lax.rem(y + dy, 4))

    def along_z(dz):
        return (lax.rem(z + dz, 4) * 2 + c, l)

    sibling = (z * 2 + other, l)

    def quarter(dz):
        return pl.ds(pl.multiple_of(lax.rem(z + dz, 4) * QUART, 128), QUART)

    def rows(start, size):
        return pl.ds(pl.multiple_of(start, size), size)

    def wait(ref, sem):
        pltpu.make_async_copy(ref, ref, sem).wait()

    def push(src, dst, send_sem, recv_sem, device):
        pltpu.make_async_remote_copy(
            src_ref=src, dst_ref=dst, send_sem=send_sem, recv_sem=recv_sem,
            device_id=device, device_id_type=MESH,
        ).start()

    def push_or_keep(here, src, dst, send_sem, recv_sem, device):
        @pl.when(here)
        def _():
            pltpu.make_async_copy(src, dst, recv_sem).start()

        @pl.when(jnp.logical_not(here))
        def _():
            push(src, dst, send_sem, recv_sem, device)

    barrier = pltpu.get_barrier_semaphore()
    for dx in range(4):
        for dy in range(4):
            if (dx, dy) != (0, 0):
                pl.semaphore_signal(barrier, inc=1, device_id=plane(dx, dy), device_id_type=MESH)
    for dz in (1, 2, 3):
        pl.semaphore_signal(barrier, inc=1, device_id=along_z(dz), device_id_type=MESH)
    pl.semaphore_signal(barrier, inc=1, device_id=sibling, device_id_type=MESH)

    for h in (0, 1):
        place = tok.at[:, pl.ds(h * QUART, QUART)]

        @pl.when(c == 0)
        def _():
            pltpu.make_async_copy(saved.at[:, quarter(h)], place, load_sem.at[0]).start()

        @pl.when(c == 1)
        def _():
            pltpu.make_async_copy(ograd.at[:, quarter(h)], place, load_sem.at[0]).start()

    pltpu.make_async_copy(gate_w, w.at[:, pl.ds(0, HID)], load_sem.at[1]).start()
    pltpu.make_async_copy(up_w, w.at[:, pl.ds(HID, HID)], load_sem.at[1]).start()
    pltpu.make_async_copy(down_w, wd, load_sem.at[2]).start()

    expert_lane = lax.broadcasted_iota(jnp.int32, (TOK, 128), 1)
    first = jnp.where(routes[:, 0:1] == expert_lane, 1.0, 0.0)
    second = jnp.where(routes[:, 1:2] == expert_lane, 1.0, 0.0)
    lower = jnp.where(
        lax.broadcasted_iota(jnp.int32, (TOK, TOK), 1) < lax.broadcasted_iota(jnp.int32, (TOK, TOK), 0), 1.0, 0.0
    ).astype(BF16)
    earlier = dot(lower, (first + second).astype(BF16), ((1,), (0,)))
    target0 = routes[:, 0:1].astype(F32) * CAP + jnp.sum(earlier * first, axis=1, keepdims=True)
    target1 = routes[:, 1:2].astype(F32) * CAP + jnp.sum(earlier * second, axis=1, keepdims=True)

    def slot_numbers(j):
        lane = lax.broadcasted_iota(jnp.int32, (1, CHUNK), 1)
        i = lax.div(lane, CAP)
        expert = lax.rem(x + i, 4) * 4 + lax.rem(y + i + j, 4)
        return (expert * CAP + lax.rem(lane, CAP)).astype(F32)

    for j in range(4):
        number = slot_numbers(j)
        hit0, hit1 = target0 == number, target1 == number
        onehot[:, j * CHUNK:(j + 1) * CHUNK] = jnp.where(hit0 | hit1, 1.0, 0.0).astype(BF16)
        weight = jnp.where(hit0, gates[:, 0:1].astype(F32), 0.0) + jnp.where(hit1, gates[:, 1:2].astype(F32), 0.0)
        gsend[:, j * CHUNK:(j + 1) * CHUNK] = jnp.broadcast_to(jnp.sum(weight, axis=0, keepdims=True), (8, CHUNK))

    wait(tok, load_sem.at[0])

    def pick(j):
        picked = dot(onehot[:, rows(j * CHUNK, CHUNK)], tok[...], ((0,), (0,)))
        send[rows(j * CHUNK, CHUNK), :] = picked.astype(BF16)

    def dispatch(j):
        for i in range(4):
            block = j * 4 + i
            device = plane(i, i + j)
            tile = gsend.at[:, rows(j * CHUNK + (i // 2) * 128, 128)]
            here = rows(block * CAP, CAP)
            copies = [(tile, grecv.at[block], gate_send, gate_recv)]
            for h in (0, 1):
                copies.append((
                    send.at[here, pl.ds(h * QUART, QUART)], xy.at[c, here, quarter(h)], disp_send, disp_recv.at[j, h],
                ))
            for src, dst, ssem, rsem in copies:
                if i == 0:
                    push_or_keep(j == 0, src, dst, ssem, rsem, device)
                else:
                    push(src, dst, ssem, rsem, device)

    pick(0)
    pl.semaphore_wait(barrier, 19)
    dispatch(0)

    @pl.loop(1, 4)
    def _(j):
        pick(j)
        dispatch(j)

    def forward(j):
        here = rows(j * CHUNK, CHUNK)
        for h, dz in ((0, 1), (1, 3)):
            block = xy.at[c, here, quarter(h)]
            wait(block, disp_recv.at[j, h])
            push(block, block, fz_send, fz_recv.at[j, h], along_z(dz))
            push(block, block, fs_send, fs_recv.at[j, h], sibling)

    def hand_over(j):
        here = rows(j * CHUNK, CHUNK)
        for h, dz in ((0, 3), (1, 2)):
            block = xy.at[c, here, quarter(dz)]
            wait(block, fz_recv.at[j, h])
            push(block, block, fs_send, fs_recv.at[j, 2 + h], sibling)

    def compute(j):
        here = rows(j * CHUNK, CHUNK)
        slot = lax.rem(j, 2)
        for h, dz in ((0, 0), (1, 1), (2, 3), (3, 2)):
            wait(xy.at[other, here, quarter(dz)], fs_recv.at[j, h])

        @pl.when(j == 0)
        def _():
            wait(grecv, gate_recv)
            wait(w, load_sem.at[1])
            wait(wd, load_sem.at[2])

        lane = lax.broadcasted_iota(jnp.int32, (CAP, 128), 1)
        row = lax.broadcasted_iota(jnp.int32, (CAP, 128), 0)
        cols = []
        for i in range(4):
            values = grecv[j * 4 + i][0:1, :]
            cols.append(jnp.sum(jnp.where(lane == row + (i % 2) * CAP, values, 0.0), axis=1, keepdims=True))
        gate = jnp.concatenate(cols, axis=0)
        pre = dot(xy[0, here, :], w[...], ((1,), (0,)))
        back_proj = dot(xy[1, here, :], wd[...], ((1,), (1,)))
        gate_pre, up_pre = pre[:, :HID], pre[:, HID:]
        sig = jax.nn.sigmoid(gate_pre)
        act = gate_pre * sig
        act_up = act * up_pre
        term = jnp.sum(act_up * back_proj, axis=1, keepdims=True)
        hidden[here, :] = (gate * act_up).astype(BF16)
        hidden_grad = gate * back_proj
        grad_pre[here, 0:HID] = (hidden_grad * up_pre * sig * (1.0 + gate_pre * (1.0 - sig))).astype(BF16)
        grad_pre[here, HID:2 * HID] = (hidden_grad * act).astype(BF16)

        eye = lax.broadcasted_iota(jnp.int32, (CHUNK, CHUNK), 0) == lax.broadcasted_iota(jnp.int32, (CHUNK, CHUNK), 1)
        term_row = jnp.sum(jnp.where(eye, term, 0.0), axis=0, keepdims=True)
        gt_send[:, here] = jnp.broadcast_to(term_row, (8, CHUNK))
        for i in range(4):
            device = plane(4 - i, 8 - i - j)
            tile = gt_send.at[:, rows(j * CHUNK + (i // 2) * 128, 128)]
            if i == 0:
                push_or_keep(j == 0, tile, gt_recv.at[j * 4 + i], gts_send, gts_recv, device)
            else:
                push(tile, gt_recv.at[j * 4 + i], gts_send, gts_recv, device)

        @pl.when(j >= 2)
        def _():
            wait(part.at[slot, pl.ds(0, HALF)], sib_send.at[slot])
            wait(part.at[slot, pl.ds(0, HALF), pl.ds(0, 2 * QUART)], zr_send.at[slot])

        @pl.loop(0, FEAT // TILE)
        def _(t):
            cut = rows(t * TILE, TILE)
            part[slot, :, cut] = dot(grad_pre[here, :], w[cut, :], ((1,), (1,))).astype(BF16)

        push(
            part.at[slot, rows(other * HALF, HALF)], sib_in.at[rows(j * HALF, HALF)],
            sib_send.at[slot], sib_recv.at[j], sibling,
        )

    def sum_cores(j):
        slot = lax.rem(j, 2)
        mine, here = rows(c * HALF, HALF), rows(j * HALF, HALF)
        wait(sib_in.at[here], sib_recv.at[j])

        @pl.loop(0, FEAT // TILE)
        def _(t):
            cut = rows(t * TILE, TILE)
            part[slot, mine, cut] = (part[slot, mine, cut].astype(F32) + sib_in[here, cut].astype(F32)).astype(BF16)

        for h, dz in ((0, 1), (1, 3)):
            push(part.at[slot, mine, quarter(dz)], z_in.at[h, here], zr_send.at[slot], zr_recv.at[j, h], along_z(dz))
        ret[0, here, :] = part[slot, mine, quarter(0)]
        ret[1, here, :] = part[slot, mine, quarter(2)]
        send_back(j, 1)

    def send_back(j, s):
        for ii in (0, 1):
            i = 2 * c + ii
            here = rows(j * HALF + ii * CAP, CAP)
            device = plane(4 - i, 8 - i - j)
            args = (ret.at[s, here], back.at[s, here], ret_send, ret_recv.at[s], device)
            if ii == 0:
                push_or_keep((j == 0) & (c == 0), *args)
            else:
                push(*args)

    def sum_planes(j):
        here = rows(j * HALF, HALF)
        for h in (0, 1):
            wait(z_in.at[h, here], zr_recv.at[j, h])
        ret[0, here, :] = (
            ret[0, here, :].astype(F32) + z_in[0, here, :].astype(F32) + z_in[1, here, :].astype(F32)
        ).astype(BF16)
        send_back(j, 0)

    def weight_grads(j):
        here = rows(j * CHUNK, CHUNK)
        turned = hidden[here, :].T

        @pl.loop(0, FEAT // TILE)
        def _(t):
            cut = rows(t * TILE, TILE)
            gu = dot(xy[0, here, cut], grad_pre[here, :], ((0,), (0,)))
            down = dot(turned, xy[1, here, cut], ((1,), (0,)))

            @pl.when(j == 0)
            def _():
                dw_gu[cut, :] = gu
                dw_d[:, cut] = down

            @pl.when(j > 0)
            def _():
                dw_gu[cut, :] += gu
                dw_d[:, cut] += down

    forward(0)

    @pl.loop(0, 4)
    def _(j):
        @pl.when(j < 3)
        def _():
            forward(j + 1)

        hand_over(j)
        compute(j)
        sum_cores(j)

        @pl.when(j > 0)
        def _():
            sum_planes(j - 1)

        weight_grads(j)

    outs = (
        (dw_gu.at[:, pl.ds(0, HID)], ggw_o), (dw_gu.at[:, pl.ds(HID, HID)], guw_o), (dw_d, gdw_o),
    )
    for i, (src, dst) in enumerate(outs):
        pltpu.make_async_copy(src, dst, out_sem.at[i]).start()
    sum_planes(3)

    wait(gt_recv, gts_recv)
    low = lax.broadcasted_iota(jnp.int32, (8, 128), 1) < CAP
    for m in range(8):
        gt_mine[:, m * 128:(m + 1) * 128] = jnp.where(low, gt_recv[2 * m], gt_recv[2 * m + 1])
    push(gt_mine, gt_sib, gtx_send, gtx_recv, sibling)

    def combine(s):
        total = jnp.zeros((TOK, QUART), F32)
        for j in range(4):
            hits = onehot[:, rows(j * CHUNK + c * HALF, HALF)]
            total += dot(hits, back[s, j * HALF:(j + 1) * HALF, :], ((1,), (0,)))
        comb[s, :, :] = total

    def window(core):
        return pl.ds(pl.multiple_of(core * (QUART - WIN), 128), WIN)

    wait(back.at[1], ret_recv.at[1])
    combine(1)
    push(comb.at[1, :, window(other)], comb_sib.at[1], cs_send.at[1], cs_recv.at[1], sibling)

    wait(gt_sib, gtx_recv)
    gt_z[z] = gt_mine[...] + gt_sib[...]
    for dz in (1, 2, 3):
        push(gt_z.at[z], gt_z.at[z], gtz_send.at[dz], gtz_recv.at[dz], along_z(dz))

    wait(comb_sib.at[1], cs_recv.at[1])
    opp_out[...] = (comb[1, :, window(c)] + comb_sib[1]).astype(BF16)
    push(opp_out, opp_in, op_send, op_recv, along_z(2))

    wait(back.at[0], ret_recv.at[0])
    combine(0)
    push(comb.at[0, :, window(other)], comb_sib.at[0], cs_send.at[0], cs_recv.at[0], sibling)

    for dz in (1, 2, 3):
        wait(gt_z.at[lax.rem(z + 4 - dz, 4)], gtz_recv.at[dz])
    total_row = (gt_z[0] + gt_z[1] + gt_z[2] + gt_z[3])[0:1, :]
    sum0, sum1 = jnp.zeros((TOK, 1), F32), jnp.zeros((TOK, 1), F32)
    for j in range(4):
        number = slot_numbers(j)
        term = total_row[:, j * CHUNK:(j + 1) * CHUNK]
        sum0 += jnp.sum(jnp.where(target0 == number, term, 0.0), axis=1, keepdims=True)
        sum1 += jnp.sum(jnp.where(target1 == number, term, 0.0), axis=1, keepdims=True)
    gg_o[:, 0:1] = sum0
    gg_o[:, 1:2] = sum1

    wait(comb_sib.at[0], cs_recv.at[0])
    wait(opp_in, op_recv)
    result = (comb[0, :, window(c)] + comb_sib[0] + opp_in[...].astype(F32)).astype(BF16)

    @pl.when(c == 0)
    def _():
        gin_o[...] = result[:, 0:QUART // 2]

    @pl.when(c == 1)
    def _():
        gin_o[...] = result[:, WIN - QUART // 2:WIN]

    for i, (src, dst) in enumerate(outs):
        pltpu.make_async_copy(src, dst, out_sem.at[i]).wait()
    wait(send.at[pl.ds(CAP, ROWS - CAP)], disp_send)
    wait(grecv.at[pl.ds(1, 15)], gate_send)
    wait(gt_recv.at[pl.ds(1, 15)], gts_send)
    wait(send, fz_send)
    wait(xy.at[c], fs_send)
    for slot in (0, 1):
        wait(part.at[slot, pl.ds(0, HALF)], sib_send.at[slot])
        wait(part.at[slot, pl.ds(0, HALF), pl.ds(0, 2 * QUART)], zr_send.at[slot])

    @pl.when(c == 0)
    def _():
        wait(ret.at[0, pl.ds(CAP, 512 - CAP)], ret_send)
        wait(ret.at[1, pl.ds(CAP, 512 - CAP)], ret_send)

    @pl.when(c == 1)
    def _():
        wait(ret.at[0], ret_send)
        wait(ret.at[1], ret_send)

    wait(gt_mine, gtx_send)
    for dz in (1, 2, 3):
        wait(gt_z.at[z], gtz_send.at[dz])
    for s in (0, 1):
        wait(comb_sib.at[s], cs_send.at[s])
    wait(opp_out, op_send)


def on_device(saved_input, out_grad, routes, gates, gate_weight, up_weight, down_weight):
    anywhere = pl.BlockSpec(memory_space=pl.ANY)
    vmem = pl.BlockSpec(memory_space=pltpu.VMEM)
    dma = pltpu.SemaphoreType.DMA
    scratch = [
        pltpu.VMEM((TOK, 2 * QUART), BF16),
        pltpu.VMEM((ROWS, 2 * QUART), BF16),
        pltpu.VMEM((TOK, ROWS), BF16),
        pltpu.VMEM((8, ROWS), F32),
        pltpu.VMEM((16, 8, 128), F32),
        pltpu.VMEM((2, ROWS, FEAT), BF16),
        pltpu.VMEM((FEAT, 2 * HID), BF16),
        pltpu.VMEM((HID, FEAT), BF16),
        pltpu.VMEM((ROWS, 2 * HID), BF16),
        pltpu.VMEM((ROWS, HID), BF16),
        pltpu.VMEM((2, CHUNK, FEAT), BF16),
        pltpu.VMEM((ROWS // 2, FEAT), BF16),
        pltpu.VMEM((2, ROWS // 2, QUART), BF16),
        pltpu.VMEM((2, ROWS // 2, QUART), BF16),
        pltpu.VMEM((2, ROWS // 2, QUART), BF16),
        pltpu.VMEM((8, ROWS), F32),
        pltpu.VMEM((16, 8, 128), F32),
        pltpu.VMEM((8, ROWS), F32),
        pltpu.VMEM((8, ROWS), F32),
        pltpu.VMEM((4, 8, ROWS), F32),
        pltpu.VMEM((2, TOK, QUART), F32),
        pltpu.VMEM((2, TOK, WIN), F32),
        pltpu.VMEM((TOK, WIN), BF16),
        pltpu.VMEM((TOK, WIN), BF16),
        pltpu.VMEM((FEAT, 2 * HID), F32),
        pltpu.VMEM((HID, FEAT), F32),
        dma((3,)),
        dma(()), dma((4, 2)),
        dma(()), dma(()),
        dma(()), dma((4, 2)),
        dma(()), dma((4, 4)),
        dma((2,)), dma((4,)),
        dma((2,)), dma((4, 2)),
        dma(()), dma((2,)),
        dma(()), dma(()),
        dma(()), dma(()),
        dma((4,)), dma((4,)),
        dma((2,)), dma((2,)),
        dma(()), dma(()),
        dma((3,)),
    ]
    gin, gg, ggw, guw, gdw = pl.pallas_call(
        kernel,
        out_shape=(
            jax.ShapeDtypeStruct((TOK, QUART // 2), BF16),
            jax.ShapeDtypeStruct((TOK, 2), F32),
            jax.ShapeDtypeStruct((FEAT, HID), F32),
            jax.ShapeDtypeStruct((FEAT, HID), F32),
            jax.ShapeDtypeStruct((HID, FEAT), F32),
        ),
        in_specs=[anywhere, anywhere, vmem, vmem, anywhere, anywhere, anywhere],
        out_specs=(vmem, vmem, anywhere, anywhere, anywhere),
        scratch_shapes=scratch,
        compiler_params=pltpu.CompilerParams(
            collective_id=0, has_side_effects=True, vmem_limit_bytes=62 * 2**20
        ),
        cost_estimate=pl.CostEstimate(flops=15 * 10**9, bytes_accessed=20 * 10**6, transcendentals=10**6),
    )(saved_input, out_grad, routes, gates, gate_weight[0], up_weight[0], down_weight[0])
    return gin, gg, ggw[None], guw[None], gdw[None]


def solution(mesh):
    placed = (
        P("local", None),
        P("local", None),
        P("local", None),
        P("local", None),
        P("local", None, "node"),
        P("local", None, "node"),
        P("local", "node", None),
    )
    return jax.shard_map(
        on_device,
        mesh=mesh,
        in_specs=placed,
        out_specs=(
            P("local", "node"),
            P("local", None),
            P("local", None, "node"),
            P("local", None, "node"),
            P("local", "node", None),
        ),
        check_vma=False,
    )
```

time: 684 us -> 140 us (0.20)
  waiting for transfers between devices: 462 us -> 0 us
  Pallas kernels: 0 us -> 122 us
  local copies, waits for them, and re-layouts: 84 us -> 15.7 us
  starting transfers between devices: 40.6 us -> 0 us
  matrix products: 39.4 us -> 0 us
  blocking collectives: 20.4 us -> 0 us
  other arithmetic: 16.7 us -> 0 us
  between operations: 14.5 us -> 0.64 us
    all_to_all x5 -> x0, waiting for transfers between devices: 435 us -> none  [the longest x1 248 us: on_device(): lax.all_to_all(partial_value.reshape(experts, capacity, features), 'local...]
    pallas_call x0 -> x1, Pallas kernels: none -> 122 us  [on_device(): pl.pallas_call(kernel, out_shape=(jax.ShapeDtypeStruct((TOK, QUART // 2),...]
    scatter x3 -> x0, local copies, waits for them, and re-layouts: 43.2 us -> none  [the longest x1 20.7 us: on_device(): send_input = jnp.zeros((slot_rows, features), jnp.bfloat16).at[target].se...]
    all_to_all x5 -> x0, starting transfers between devices: 40.6 us -> none  [the longest x1 11.5 us: on_device(): lax.all_to_all(send_grad, 'local', split_axis=0, concat_axis=0, tiled=True)]
    dot_general x5 -> x0, matrix products: 39.4 us -> none  [the longest x1 9.42 us: on_device(): lax.dot_general(grad_pre_both, gate_both, contract_feat, preferred_elemen...]
    unnamed x2 -> x0, waiting for transfers between devices: 26.3 us -> none
    gather x4 -> x0, local copies, waits for them, and re-layouts: 25.3 us -> none  [the longest x2 22.6 us: pick_rows(): picked = jnp.take(table, target, axis=0)]
    psum x1 -> x0, blocking collectives: 20.4 us -> none  [on_device(): gate_sum = lax.psum(gate_term, 'node').reshape(experts, capacity)]
  transfers between devices with their start and end apart: 6 -> 0, of which waited for: 4 -> 0; matrix products, arithmetic and copies ran while one was open for 12% -> 0% of each run, Pallas kernels for 0% -> 0%
where the time goes in v1:
time: 140 us; the launch traced here: 138 us
  Pallas kernels  122 us (87%)
  local copies, waits for them, and re-layouts  15.7 us (11%)
    pallas_call x1, Pallas kernels, on_device(): pl.pallas_call(kernel, out_shape=(jax.ShapeDtypeStruct((TOK, QUART // 2),...  122 us
    unnamed x11, local copies, waits for them, and re-layouts  15.7 us

profile of v1, /device:TPU:1, one launch (start us, length us, event | category | flops | bytes accessed | tf_op | source)
XLA Modules:
  0.0 138.3 jit_solution(14713888546910616980)
XLA Ops:
  0.6 1.4 %copy.13.gates = bf16[256,2]{1,0:T(8,128)(2,1)} copy(bf16[256,2]{0,1:T(2,128)(2,1)} %param.10) | data formatting | bytes 2048 | tf_op args[3]
  2.1 1.5 %copy.12.routes = s32[256,2]{1,0:T(8,128)} copy(s32[256,2]{0,1:T(2,128)} %param.9) | data formatting | bytes 4096 | tf_op args[2]
  3.5 121.9 %shard_map.110 = (bf16[256,448]{1,0:T(8,128)(2,1)}, f32[256,2]{1,0:T(8,128)}, f32[3584,256]{1,0:T(8,128)}, f32[3584,256]{1,0:T(8,128)}, f32[256,3584]{1,0:T(8,128)}) custom-call(bf16[256,3584]{1,0:T(8,128)(2,1)} %saved.1, bf16[256,3584]{1,0:T(8,128)(2,1)} %ograd.1, s32[256,2]{1,0:T(8,128)} %copy.12.routes, bf16[256,2]{1,0:T(8,128)(2,1)} %copy.13.gates, ...), custom_call_target="tpu_custom_call" | custom-call | flops 15000000512 | bytes 20000000 | tf_op jit(solution)/shard_map/pallas_call | solution.py:440
  125.5 1.8 %copy.14 = bf16[256,448]{0,1:T(8,128)(2,1)} copy(bf16[256,448]{1,0:T(8,128)(2,1)} %get-tuple-element.15) | data formatting | bytes 458752
  127.2 1.6 %copy.15 = f32[256,2]{0,1:T(2,128)} copy(f32[256,2]{1,0:T(8,128)} %get-tuple-element.16) | data formatting | bytes 4096
  128.8 0.0 copy-start.1
  128.8 4.3 %copy.19 = f32[1,3584,256]{2,1,0:T(8,128)} copy(f32[1,3584,256]{2,1,0:T(8,128)} %bitcast.8) | data formatting | bytes 7340032
  133.1 0.0 copy-done.1
  133.1 0.0 copy-start
  133.1 1.9 %copy.20 = f32[1,3584,256]{2,1,0:T(8,128)} copy(f32[1,3584,256]{2,1,0:T(8,128)S(1)} %bitcast.7) | data formatting | bytes 7340032
  134.9 1.5 %copy-done = f32[256,3584]{1,0:T(8,128)S(1)} copy-done((f32[256,3584]{1,0:T(8,128)S(1)}, f32[256,3584]{1,0:T(8,128)}, u32[]{:S(2)}) %copy-start) | copy-done | bytes 3670040
  136.4 1.8 %copy.21 = f32[1,256,3584]{2,1,0:T(8,128)} copy(f32[1,256,3584]{2,1,0:T(8,128)S(1)} %bitcast.6) | data formatting | bytes 7340032
Async XLA Ops:
  128.8 4.3 %copy-start.1 = (f32[3584,256]{1,0:T(8,128)S(1)}, f32[3584,256]{1,0:T(8,128)}, u32[]{:S(2)}) copy-start(f32[3584,256]{1,0:T(8,128)} %get-tuple-element.13) | copy-start | bytes 11010052
  133.1 3.4 %copy-start = (f32[256,3584]{1,0:T(8,128)S(1)}, f32[256,3584]{1,0:T(8,128)}, u32[]{:S(2)}) copy-start(f32[256,3584]{1,0:T(8,128)} %get-tuple-element.14) | copy-start | bytes 11010052

commit v2 on v1

v2 whole, which is shorter than its diff:
```python
import functools

import jax
import jax.numpy as jnp
from jax import lax
from jax.experimental import pallas as pl
from jax.experimental.pallas import tpu as pltpu
from jax.sharding import PartitionSpec as P

MESH = pl.DeviceIdType.MESH
F32 = jnp.float32
BF16 = jnp.bfloat16
TOK = 256
FEAT = 3584
QUART = FEAT // 4
HID = 256
CAP = 64
ROWS = 16 * CAP
CHUNK = 4 * CAP
HALF = CHUNK // 2
WIN = 512
TILE = 512

OFFSETS = (
    ((0, 1), (0, 3), (1, 0), (3, 0)),
    ((0, 0), (2, 2), (2, 0), (0, 2)),
    ((1, 1), (3, 3), (1, 3), (3, 1)),
    ((1, 2), (3, 2), (2, 1), (2, 3)),
)
SELF = (1, 0)


def dot(a, b, dims):
    return lax.dot_general(a, b, (dims, ((), ())), preferred_element_type=F32)


def eye(size):
    return lax.broadcasted_iota(jnp.int32, (size, size), 0) == lax.broadcasted_iota(jnp.int32, (size, size), 1)


def column(row):
    return jnp.sum(jnp.where(eye(TOK), row, 0.0), axis=1, keepdims=True)


def as_row(col):
    return jnp.sum(jnp.where(eye(TOK), col, 0.0), axis=0, keepdims=True)


def kernel(
    saved, ograd, routes, gates, gate_w, up_w, down_w,
    gin_o, gg_o, ggw_o, guw_o, gdw_o,
    tok, send, onehot, gsend, grecv, xy, w, wd, grad_pre, hidden, part,
    sib_in, z_in, ret, back, gt_send, gt_recv, gt_sib, gt_mine, gt_z,
    comb, comb_sib, opp_out, opp_in, dw_gu, dw_d, stage_gu, stage_d,
    load_sem, disp_send, disp_recv, gate_send, gate_recv, fz_send, fz_recv, fs_send, fs_recv,
    sib_send, sib_recv, zr_send, zr_recv, ret_send, ret_recv, gts_send, gts_recv, gtx_send, gtx_recv,
    gtz_send, gtz_recv, cs_send, cs_recv, op_send, op_recv, out_sem,
):
    n, l = lax.axis_index("node"), lax.axis_index("local")
    z, c = lax.div(n, 2), lax.rem(n, 2)
    x, y = lax.div(l, 4), lax.rem(l, 4)
    other = 1 - c

    def plane(dx, dy):
        return (n, lax.rem(x + dx, 4) * 4 + lax.rem(y + dy, 4))

    def along_z(dz):
        return (lax.rem(z + dz, 4) * 2 + c, l)

    sibling = (z * 2 + other, l)

    def quarter(dz):
        return pl.ds(pl.multiple_of(lax.rem(z + dz, 4) * QUART, 128), QUART)

    def rows(start, size):
        return pl.ds(pl.multiple_of(start, size), size)

    def wait(ref, sem):
        pltpu.make_async_copy(ref, ref, sem).wait()

    def push(src, dst, send_sem, recv_sem, device):
        pltpu.make_async_remote_copy(
            src_ref=src, dst_ref=dst, send_sem=send_sem, recv_sem=recv_sem,
            device_id=device, device_id_type=MESH,
        ).start()

    barrier = pltpu.get_barrier_semaphore()
    for dx in range(4):
        for dy in range(4):
            if (dx, dy) != (0, 0):
                pl.semaphore_signal(barrier, inc=1, device_id=plane(dx, dy), device_id_type=MESH)
    for dz in (1, 2, 3):
        pl.semaphore_signal(barrier, inc=1, device_id=along_z(dz), device_id_type=MESH)
    pl.semaphore_signal(barrier, inc=1, device_id=sibling, device_id_type=MESH)

    for h in (0, 1):
        place = tok.at[:, pl.ds(h * QUART, QUART)]

        @pl.when(c == 0)
        def _():
            pltpu.make_async_copy(saved.at[:, quarter(h)], place, load_sem.at[0]).start()

        @pl.when(c == 1)
        def _():
            pltpu.make_async_copy(ograd.at[:, quarter(h)], place, load_sem.at[0]).start()

    pltpu.make_async_copy(gate_w, w.at[:, pl.ds(0, HID)], load_sem.at[1]).start()
    pltpu.make_async_copy(up_w, w.at[:, pl.ds(HID, HID)], load_sem.at[1]).start()
    pltpu.make_async_copy(down_w, wd, load_sem.at[2]).start()

    route0, route1 = column(routes[0:1, :].astype(F32)), column(routes[1:2, :].astype(F32))
    gate0, gate1 = column(gates[0:1, :].astype(F32)), column(gates[1:2, :].astype(F32))
    expert_lane = lax.broadcasted_iota(jnp.int32, (TOK, 128), 1).astype(F32)
    first = jnp.where(route0 == expert_lane, 1.0, 0.0)
    second = jnp.where(route1 == expert_lane, 1.0, 0.0)
    lower = jnp.where(
        lax.broadcasted_iota(jnp.int32, (TOK, TOK), 1) < lax.broadcasted_iota(jnp.int32, (TOK, TOK), 0), 1.0, 0.0
    ).astype(BF16)
    earlier = dot(lower, (first + second).astype(BF16), ((1,), (0,)))
    target0 = route0 * CAP + jnp.sum(earlier * first, axis=1, keepdims=True)
    target1 = route1 * CAP + jnp.sum(earlier * second, axis=1, keepdims=True)

    def slot_numbers(j):
        lane = lax.broadcasted_iota(jnp.int32, (1, CHUNK), 1)
        which, number = lax.div(lane, CAP), lax.rem(lane, CAP)
        for i, (dx, dy) in enumerate(OFFSETS[j]):
            expert = lax.rem(x + dx, 4) * 4 + lax.rem(y + dy, 4)
            number = number + jnp.where(which == i, expert * CAP, 0)
        return number.astype(F32)

    def mark(j):
        number = slot_numbers(j)
        hit0, hit1 = target0 == number, target1 == number
        onehot[:, j * CHUNK:(j + 1) * CHUNK] = jnp.where(hit0 | hit1, 1.0, 0.0).astype(BF16)
        weight = jnp.where(hit0, gate0, 0.0) + jnp.where(hit1, gate1, 0.0)
        gsend[:, j * CHUNK:(j + 1) * CHUNK] = jnp.broadcast_to(jnp.sum(weight, axis=0, keepdims=True), (8, CHUNK))

    def pick(j):
        picked = dot(onehot[:, j * CHUNK:(j + 1) * CHUNK], tok[...], ((0,), (0,)))
        send[j * CHUNK:(j + 1) * CHUNK, :] = picked.astype(BF16)

    def send_gates(j):
        for i, (dx, dy) in enumerate(OFFSETS[j]):
            tile = gsend.at[:, pl.ds(j * CHUNK + (i // 2) * 128, 128)]
            if (j, i) == SELF:
                pltpu.make_async_copy(tile, grecv.at[j * 4 + i], gate_recv).start()
            else:
                push(tile, grecv.at[j * 4 + i], gate_send, gate_recv, plane(dx, dy))

    def dispatch(j, h, p=None):
        for i, (dx, dy) in enumerate(OFFSETS[j]):
            if p is not None and i // 2 != p:
                continue
            here = pl.ds((j * 4 + i) * CAP, CAP)
            src, dst = send.at[here, pl.ds(h * QUART, QUART)], xy.at[c, here, quarter(h)]
            rsem = disp_recv.at[j + (p or 0), h]
            if (j, i) == SELF:
                pltpu.make_async_copy(src, dst, rsem).start()
            else:
                push(src, dst, disp_send, rsem, plane(dx, dy))

    def forward(j, h, p=None):
        here = pl.ds(j * CHUNK, CHUNK) if p is None else pl.ds(j * CHUNK + p * HALF, HALF)
        block = xy.at[c, here, quarter(h)]
        wait(block, disp_recv.at[j + (p or 0), h])
        push(block, block, fz_send, fz_recv.at[j, h], along_z((1, 3)[h]))
        push(block, block, fs_send, fs_recv.at[j, h], sibling)

    def hand_over(j):
        here = pl.ds(j * CHUNK, CHUNK)
        for h, dz in ((0, 3), (1, 2)):
            block = xy.at[c, here, quarter(dz)]
            wait(block, fz_recv.at[j, h])
            push(block, block, fs_send, fs_recv.at[j, 2 + h], sibling)

    def compute(j):
        here = pl.ds(j * CHUNK, CHUNK)
        slot = j % 2
        for h, dz in ((0, 0), (1, 1), (2, 3), (3, 2)):
            wait(xy.at[other, here, quarter(dz)], fs_recv.at[j, h])
        lane = lax.broadcasted_iota(jnp.int32, (CAP, 128), 1)
        row = lax.broadcasted_iota(jnp.int32, (CAP, 128), 0)
        cols = []
        for i in range(4):
            values = grecv[j * 4 + i][0:1, :]
            cols.append(jnp.sum(jnp.where(lane == row + (i % 2) * CAP, values, 0.0), axis=1, keepdims=True))
        gate = jnp.concatenate(cols, axis=0)
        pre = dot(xy[0, here, :], w[...], ((1,), (0,)))
        back_proj = dot(xy[1, here, :], wd[...], ((1,), (1,)))
        gate_pre, up_pre = pre[:, :HID], pre[:, HID:]
        sig = jax.nn.sigmoid(gate_pre)
        act = gate_pre * sig
        act_up = act * up_pre
        term = jnp.sum(act_up * back_proj, axis=1, keepdims=True)
        hidden[here, :] = (gate * act_up).astype(BF16)
        hidden_grad = gate * back_proj
        grad_pre[here, 0:HID] = (hidden_grad * up_pre * sig * (1.0 + gate_pre * (1.0 - sig))).astype(BF16)
        grad_pre[here, HID:2 * HID] = (hidden_grad * act).astype(BF16)
        gt_send[:, here] = jnp.broadcast_to(as_row(term), (8, CHUNK))

        if j >= 2:
            wait(part.at[slot, pl.ds(0, HALF)], sib_send.at[slot])
            wait(part.at[slot, pl.ds(0, HALF), pl.ds(0, 2 * QUART)], zr_send.at[slot])
        for dz in (1, 3, 2, 0):
            cut = quarter(dz)
            part[slot, :, cut] = dot(grad_pre[here, :], w[cut, :], ((1,), (1,))).astype(BF16)
            push(
                part.at[slot, rows(other * HALF, HALF), cut], sib_in.at[pl.ds(j * HALF, HALF), cut],
                sib_send.at[slot], sib_recv.at[j, dz], sibling,
            )
        for i, (dx, dy) in enumerate(OFFSETS[j]):
            tile = gt_send.at[:, pl.ds(j * CHUNK + (i // 2) * 128, 128)]
            if (j, i) == SELF:
                pltpu.make_async_copy(tile, gt_recv.at[j * 4 + i], gts_recv).start()
            else:
                push(tile, gt_recv.at[j * 4 + i], gts_send, gts_recv, plane(4 - dx, 4 - dy))

    def sum_cores(j):
        slot = j % 2
        mine, here = rows(c * HALF, HALF), pl.ds(j * HALF, HALF)
        for h, dz in ((0, 1), (1, 3)):
            cut = quarter(dz)
            wait(sib_in.at[here, cut], sib_recv.at[j, dz])
            part[slot, mine, cut] = (part[slot, mine, cut].astype(F32) + sib_in[here, cut].astype(F32)).astype(BF16)
            push(part.at[slot, mine, cut], z_in.at[h, here], zr_send.at[slot], zr_recv.at[j, h], along_z(dz))
        cut = quarter(2)
        wait(sib_in.at[here, cut], sib_recv.at[j, 2])
        ret[1, here, :] = (part[slot, mine, cut].astype(F32) + sib_in[here, cut].astype(F32)).astype(BF16)
        send_back(j, 1)

    def send_back(j, s):
        for ii in (0, 1):
            (dx0, dy0), (dx1, dy1) = OFFSETS[j][ii], OFFSETS[j][2 + ii]
            device = plane(4 - dx0 + c * (dx0 - dx1), 4 - dy0 + c * (dy0 - dy1))
            here = pl.ds(j * HALF + ii * CAP, CAP)
            src, dst, rsem = ret.at[s, here], back.at[s, here], ret_recv.at[s, j]
            if (j, ii) == SELF:
                @pl.when(c == 0)
                def _():
                    pltpu.make_async_copy(src, dst, rsem).start()

                @pl.when(c == 1)
                def _():
                    push(src, dst, ret_send, rsem, device)
            else:
                push(src, dst, ret_send, rsem, device)

    def sum_planes(j):
        slot = j % 2
        mine, here = rows(c * HALF, HALF), pl.ds(j * HALF, HALF)
        cut = quarter(0)
        wait(sib_in.at[here, cut], sib_recv.at[j, 0])
        total = part[slot, mine, cut].astype(F32) + sib_in[here, cut].astype(F32)
        for h in (0, 1):
            wait(z_in.at[h, here], zr_recv.at[j, h])
        ret[0, here, :] = (total + z_in[0, here, :].astype(F32) + z_in[1, here, :].astype(F32)).astype(BF16)
        send_back(j, 0)

    def weight_grads(j):
        here = pl.ds(j * CHUNK, CHUNK)
        turned = hidden[here, :].T

        @pl.loop(0, FEAT // TILE)
        def _(t):
            cut = rows(t * TILE, TILE)
            gu = dot(xy[0, here, cut], grad_pre[here, :], ((0,), (0,)))
            down = dot(turned, xy[1, here, cut], ((1,), (0,)))
            if j == 0:
                dw_gu[cut, :] = gu
                dw_d[:, cut] = down
            elif j < 3:
                dw_gu[cut, :] += gu
                dw_d[:, cut] += down
            else:
                stage_gu[cut, :] = (dw_gu[cut, :] + gu).astype(BF16)
                stage_d[:, cut] = (dw_d[:, cut] + down).astype(BF16)

    def combine(s, j):
        here = pl.ds(j * HALF, HALF)
        wait(back.at[s, here], ret_recv.at[s, j])
        total = dot(onehot[:, rows(j * CHUNK + c * HALF, HALF)], back[s, here, :], ((1,), (0,)))
        if j == 0:
            comb[s, :, :] = total
        else:
            comb[s, :, :] += total

    def window(core):
        return pl.ds(pl.multiple_of(core * (QUART - WIN), 128), WIN)

    def trade(s):
        push(comb.at[s, :, window(other)], comb_sib.at[s], cs_send.at[s], cs_recv.at[s], sibling)

    for j in range(4):
        mark(j)
    wait(tok, load_sem.at[0])
    pick(0)
    pl.semaphore_wait(barrier, 19)
    for j in range(4):
        send_gates(j)
    dispatch(0, 0)
    dispatch(0, 1)
    pick(1)
    pick(2)
    pick(3)

    forward(0, 0)
    dispatch(1, 0)
    forward(0, 1)
    dispatch(1, 1)
    forward(1, 0)
    dispatch(2, 0)
    hand_over(0)
    wait(grecv, gate_recv)
    wait(w, load_sem.at[1])
    wait(wd, load_sem.at[2])
    forward(1, 1)
    dispatch(2, 1)
    compute(0)
    forward(2, 0)
    dispatch(3, 0, 0)
    dispatch(3, 1, 0)
    sum_cores(0)
    forward(2, 1)
    hand_over(1)
    compute(1)
    forward(3, 0, 0)
    dispatch(3, 0, 1)
    sum_cores(1)
    forward(3, 1, 0)
    dispatch(3, 1, 1)
    sum_planes(0)
    hand_over(2)
    forward(3, 0, 1)
    compute(2)
    forward(3, 1, 1)
    sum_cores(2)
    sum_planes(1)
    weight_grads(0)
    hand_over(3)
    compute(3)
    sum_cores(3)
    sum_planes(2)
    weight_grads(1)
    for s in (0, 1):
        combine(s, 0)
        combine(s, 1)
    combine(1, 2)
    weight_grads(2)
    wait(gt_recv, gts_recv)
    low = lax.broadcasted_iota(jnp.int32, (8, 128), 1) < CAP
    for m in range(8):
        gt_mine[:, m * 128:(m + 1) * 128] = jnp.where(low, gt_recv[2 * m], gt_recv[2 * m + 1])
    push(gt_mine, gt_sib, gtx_send, gtx_recv, sibling)
    combine(1, 3)
    trade(1)
    sum_planes(3)
    wait(gt_sib, gtx_recv)
    gt_z[z] = gt_mine[...] + gt_sib[...]
    for dz in (1, 2, 3):
        push(gt_z.at[z], gt_z.at[z], gtz_send.at[dz], gtz_recv.at[dz], along_z(dz))
    weight_grads(3)
    outs = (
        (stage_gu.at[:, pl.ds(0, HID)], ggw_o), (stage_gu.at[:, pl.ds(HID, HID)], guw_o), (stage_d, gdw_o),
    )
    for i, (src, dst) in enumerate(outs):
        pltpu.make_async_copy(src, dst, out_sem.at[i]).start()
    wait(comb_sib.at[1], cs_recv.at[1])
    opp_out[...] = (comb[1, :, window(c)] + comb_sib[1]).astype(BF16)
    push(opp_out, opp_in, op_send, op_recv, along_z(2))
    combine(0, 2)
    combine(0, 3)
    trade(0)

    for dz in (1, 2, 3):
        wait(gt_z.at[lax.rem(z + 4 - dz, 4)], gtz_recv.at[dz])
    total_row = (gt_z[0] + gt_z[1] + gt_z[2] + gt_z[3])[0:1, :]
    sum0, sum1 = jnp.zeros((TOK, 1), F32), jnp.zeros((TOK, 1), F32)
    for j in range(4):
        number = slot_numbers(j)
        term = total_row[:, j * CHUNK:(j + 1) * CHUNK]
        sum0 += jnp.sum(jnp.where(target0 == number, term, 0.0), axis=1, keepdims=True)
        sum1 += jnp.sum(jnp.where(target1 == number, term, 0.0), axis=1, keepdims=True)
    gg_o[0:1, :] = as_row(sum0)
    gg_o[1:2, :] = as_row(sum1)

    wait(comb_sib.at[0], cs_recv.at[0])
    wait(opp_in, op_recv)
    result = (comb[0, :, window(c)] + comb_sib[0] + opp_in[...].astype(F32)).T.astype(BF16)

    @pl.when(c == 0)
    def _():
        gin_o[...] = result[0:QUART // 2, :]

    @pl.when(c == 1)
    def _():
        gin_o[...] = result[WIN - QUART // 2:WIN, :]

    for i, (src, dst) in enumerate(outs):
        pltpu.make_async_copy(src, dst, out_sem.at[i]).wait()
    wait(send.at[pl.ds(CAP, ROWS - CAP)], disp_send)
    wait(grecv.at[pl.ds(1, 15)], gate_send)
    wait(gt_recv.at[pl.ds(1, 15)], gts_send)
    wait(send, fz_send)
    wait(xy.at[c], fs_send)
    for slot in (0, 1):
        wait(part.at[slot, pl.ds(0, HALF)], sib_send.at[slot])
        wait(part.at[slot, pl.ds(0, HALF), pl.ds(0, 2 * QUART)], zr_send.at[slot])

    @pl.when(c == 0)
    def _():
        wait(ret.at[0, pl.ds(CAP, 512 - CAP)], ret_send)
        wait(ret.at[1, pl.ds(CAP, 512 - CAP)], ret_send)

    @pl.when(c == 1)
    def _():
        wait(ret.at[0], ret_send)
        wait(ret.at[1], ret_send)

    wait(gt_mine, gtx_send)
    for dz in (1, 2, 3):
        wait(gt_z.at[z], gtz_send.at[dz])
    for s in (0, 1):
        wait(comb_sib.at[s], cs_send.at[s])
    wait(opp_out, op_send)


def on_device(saved_input, out_grad, routes, gates, gate_weight, up_weight, down_weight):
    anywhere = pl.BlockSpec(memory_space=pl.ANY)
    vmem = pl.BlockSpec(memory_space=pltpu.VMEM)
    dma = pltpu.SemaphoreType.DMA
    scratch = [
        pltpu.VMEM((TOK, 2 * QUART), BF16),
        pltpu.VMEM((ROWS, 2 * QUART), BF16),
        pltpu.VMEM((TOK, ROWS), BF16),
        pltpu.VMEM((8, ROWS), F32),
        pltpu.VMEM((16, 8, 128), F32),
        pltpu.VMEM((2, ROWS, FEAT), BF16),
        pltpu.VMEM((FEAT, 2 * HID), BF16),
        pltpu.VMEM((HID, FEAT), BF16),
        pltpu.VMEM((ROWS, 2 * HID), BF16),
        pltpu.VMEM((ROWS, HID), BF16),
        pltpu.VMEM((2, CHUNK, FEAT), BF16),
        pltpu.VMEM((ROWS // 2, FEAT), BF16),
        pltpu.VMEM((2, ROWS // 2, QUART), BF16),
        pltpu.VMEM((2, ROWS // 2, QUART), BF16),
        pltpu.VMEM((2, ROWS // 2, QUART), BF16),
        pltpu.VMEM((8, ROWS), F32),
        pltpu.VMEM((16, 8, 128), F32),
        pltpu.VMEM((8, ROWS), F32),
        pltpu.VMEM((8, ROWS), F32),
        pltpu.VMEM((4, 8, ROWS), F32),
        pltpu.VMEM((2, TOK, QUART), F32),
        pltpu.VMEM((2, TOK, WIN), F32),
        pltpu.VMEM((TOK, WIN), BF16),
        pltpu.VMEM((TOK, WIN), BF16),
        pltpu.VMEM((FEAT, 2 * HID), F32),
        pltpu.VMEM((HID, FEAT), F32),
        pltpu.VMEM((FEAT, 2 * HID), BF16),
        pltpu.VMEM((HID, FEAT), BF16),
        dma((3,)),
        dma(()), dma((5, 2)),
        dma(()), dma(()),
        dma(()), dma((4, 2)),
        dma(()), dma((4, 4)),
        dma((2,)), dma((4, 4)),
        dma((2,)), dma((4, 2)),
        dma(()), dma((2, 4)),
        dma(()), dma(()),
        dma(()), dma(()),
        dma((4,)), dma((4,)),
        dma((2,)), dma((2,)),
        dma(()), dma(()),
        dma((3,)),
    ]
    gin, gg, ggw, guw, gdw = pl.pallas_call(
        kernel,
        out_shape=(
            jax.ShapeDtypeStruct((QUART // 2, TOK), BF16),
            jax.ShapeDtypeStruct((2, TOK), F32),
            jax.ShapeDtypeStruct((FEAT, HID), BF16),
            jax.ShapeDtypeStruct((FEAT, HID), BF16),
            jax.ShapeDtypeStruct((HID, FEAT), BF16),
        ),
        in_specs=[anywhere, anywhere, vmem, vmem, anywhere, anywhere, anywhere],
        out_specs=(vmem, vmem, anywhere, anywhere, anywhere),
        scratch_shapes=scratch,
        compiler_params=pltpu.CompilerParams(
            collective_id=0, has_side_effects=True, vmem_limit_bytes=62 * 2**20
        ),
        cost_estimate=pl.CostEstimate(flops=15 * 10**9, bytes_accessed=20 * 10**6, transcendentals=10**6),
    )(saved_input, out_grad, routes.T, gates.T, gate_weight[0], up_weight[0], down_weight[0])
    ggw, guw, gdw = (grad.astype(F32)[None] for grad in (ggw, guw, gdw))
    return gin.T, gg.T, ggw, guw, gdw


def solution(mesh):
    placed = (
        P("local", None),
        P("local", None),
        P("local", None),
        P("local", None),
        P("local", None, "node"),
        P("local", None, "node"),
        P("local", "node", None),
    )
    return jax.shard_map(
        on_device,
        mesh=mesh,
        in_specs=placed,
        out_specs=(
            P("local", "node"),
            P("local", None),
            P("local", None, "node"),
            P("local", None, "node"),
            P("local", "node", None),
        ),
        check_vma=False,
    )
```

time: 140 us -> 115 us (0.82)
  Pallas kernels: 122 us -> 104 us
  local copies, waits for them, and re-layouts: 15.7 us -> 1.28 us
  other arithmetic: 0 us -> 8.08 us
    pallas_call x1, Pallas kernels: 122 us -> 104 us  [on_device(): pl.pallas_call(kernel, out_shape=(jax.ShapeDtypeStruct((QUART // 2, TOK),...]
    unnamed x11 -> x8, local copies, waits for them, and re-layouts: 15.7 us -> 1.28 us
    broadcast_in_dim x0 -> x2, other arithmetic: none -> 8.08 us  [on_device(): ggw, guw, gdw = (grad.astype(F32)[None] for grad in (ggw, guw, gdw))]
where the time goes in v2:
time: 115 us; the launch traced here: 114 us
  Pallas kernels  104 us (90%)
  other arithmetic  8.08 us (7%)
  local copies, waits for them, and re-layouts  1.28 us (1%)
    pallas_call x1, Pallas kernels, on_device(): pl.pallas_call(kernel, out_shape=(jax.ShapeDtypeStruct((QUART // 2, TOK),...  104 us
    broadcast_in_dim x2, other arithmetic, on_device(): ggw, guw, gdw = (grad.astype(F32)[None] for grad in (ggw, guw, gdw))  8.08 us

profile of v2, /device:TPU:1, one launch (start us, length us, event | category | flops | bytes accessed | tf_op | source)
XLA Modules:
  0.0 114.4 jit_solution(14069250082666573892)
XLA Ops:
  0.6 104.4 %shard_map.110 = (bf16[448,256]{1,0:T(8,128)(2,1)}, f32[2,256]{1,0:T(2,128)}, bf16[3584,256]{1,0:T(8,128)(2,1)}, bf16[3584,256]{1,0:T(8,128)(2,1)}, bf16[256,3584]{1,0:T(8,128)(2,1)}) custom-call(bf16[256,3584]{1,0:T(8,128)(2,1)} %saved.1, bf16[256,3584]{1,0:T(8,128)(2,1)} %ograd.1, s32[2,256]{1,0:T(2,128)} %bitcast.21, bf16[2,256]{1,0:T(2,128)(2,1)} %bitcast.22, ...), custom_call_target="tpu_custom_call" | custom-call | flops 15000000512 | bytes 20000000 | tf_op jit(solution)/shard_map/pallas_call | solution.py:475
  105.0 0.0 copy-start
  105.0 5.8 %bitcast_convert_fusion.1 = (f32[1,3584,256]{2,1,0:T(8,128)}, f32[1,3584,256]{2,1,0:T(8,128)}) fusion(bf16[3584,256]{1,0:T(8,128)(2,1)} %get-tuple-element.13, bf16[3584,256]{1,0:T(8,128)(2,1)} %get-tuple-element.12), kind=kLoop, calls=%fused_computation.1 | loop fusion | flops 1835008 | bytes 11010048 | tf_op jit(solution)/shard_map/broadcast_in_dim | solution.py:492
  110.9 0.0 copy-done
  110.9 0.0 copy-start.1
  110.9 0.0 copy-start.2
  110.9 2.3 %bitcast_convert_fusion = f32[1,256,3584]{2,1,0:T(8,128)} fusion(bf16[256,3584]{1,0:T(8,128)(2,1)S(1)} %copy-done), kind=kLoop, calls=%fused_computation | loop fusion | flops 917504 | bytes 5505024 | tf_op jit(solution)/shard_map/broadcast_in_dim | solution.py:492
  113.1 0.0 copy-done.1
  113.1 0.7 copy.14
  113.8 0.0 copy-done.2
  113.8 0.6 copy.15
Async XLA Ops:
  105.0 5.8 %copy-start = (bf16[256,3584]{1,0:T(8,128)(2,1)S(1)}, bf16[256,3584]{1,0:T(8,128)(2,1)}, u32[]{:S(2)}) copy-start(bf16[256,3584]{1,0:T(8,128)(2,1)} %get-tuple-element.14) | copy-start | bytes 5505028
  110.9 2.3 %copy-start.1 = (bf16[448,256]{1,0:T(8,128)(2,1)S(1)}, bf16[448,256]{1,0:T(8,128)(2,1)}, u32[]{:S(2)}) copy-start(bf16[448,256]{1,0:T(8,128)(2,1)} %get-tuple-element.10) | copy-start | bytes 688132
  110.9 3.0 %copy-start.2 = (f32[2,256]{1,0:T(2,128)S(1)}, f32[2,256]{1,0:T(2,128)}, u32[]{:S(2)}) copy-start(f32[2,256]{1,0:T(2,128)} %get-tuple-element.11) | copy-start | bytes 6148

commit v3 on v2

--- a/solution.py
+++ b/solution.py
@@ -23,11 +23,11 @@
 
 OFFSETS = (
     ((0, 1), (0, 3), (1, 0), (3, 0)),
-    ((0, 0), (2, 2), (2, 0), (0, 2)),
     ((1, 1), (3, 3), (1, 3), (3, 1)),
     ((1, 2), (3, 2), (2, 1), (2, 3)),
+    ((0, 0), (2, 2), (2, 0), (0, 2)),
 )
-SELF = (1, 0)
+SELF = (3, 0)
 
 
 def dot(a, b, dims):
@@ -48,10 +48,10 @@
 
 def kernel(
     saved, ograd, routes, gates, gate_w, up_w, down_w,
-    gin_o, gg_o, ggw_o, guw_o, gdw_o,
+    gin_o, gg_o, ggu_o, gdw_o,
     tok, send, onehot, gsend, grecv, xy, w, wd, grad_pre, hidden, part,
     sib_in, z_in, ret, back, gt_send, gt_recv, gt_sib, gt_mine, gt_z,
-    comb, comb_sib, opp_out, opp_in, dw_gu, dw_d, stage_gu, stage_d,
+    comb, comb_sib, opp_out, opp_in, stage_gu, stage_d,
     load_sem, disp_send, disp_recv, gate_send, gate_recv, fz_send, fz_recv, fs_send, fs_recv,
     sib_send, sib_recv, zr_send, zr_recv, ret_send, ret_recv, gts_send, gts_recv, gtx_send, gtx_recv,
     gtz_send, gtz_recv, cs_send, cs_recv, op_send, op_recv, out_sem,
@@ -256,24 +256,18 @@
         ret[0, here, :] = (total + z_in[0, here, :].astype(F32) + z_in[1, here, :].astype(F32)).astype(BF16)
         send_back(j, 0)
 
-    def weight_grads(j):
-        here = pl.ds(j * CHUNK, CHUNK)
-        turned = hidden[here, :].T
-
-        @pl.loop(0, FEAT // TILE)
-        def _(t):
-            cut = rows(t * TILE, TILE)
-            gu = dot(xy[0, here, cut], grad_pre[here, :], ((0,), (0,)))
-            down = dot(turned, xy[1, here, cut], ((1,), (0,)))
-            if j == 0:
-                dw_gu[cut, :] = gu
-                dw_d[:, cut] = down
-            elif j < 3:
-                dw_gu[cut, :] += gu
-                dw_d[:, cut] += down
-            else:
-                stage_gu[cut, :] = (dw_gu[cut, :] + gu).astype(BF16)
-                stage_d[:, cut] = (dw_d[:, cut] + down).astype(BF16)
+    def weight_grads(t):
+        slot, cut = t % 2, pl.ds(t * TILE, TILE)
+        if t >= 2:
+            drain(slot)
+        stage_gu[slot] = dot(xy[0, :, cut], grad_pre[...], ((0,), (0,))).astype(BF16)
+        stage_d[slot] = dot(hidden[...], xy[1, :, cut], ((0,), (0,))).astype(BF16)
+        pltpu.make_async_copy(stage_gu.at[slot], ggu_o.at[cut], out_sem.at[slot, 0]).start()
+        pltpu.make_async_copy(stage_d.at[slot], gdw_o.at[:, cut], out_sem.at[slot, 1]).start()
+
+    def drain(slot):
+        wait(stage_gu.at[slot], out_sem.at[slot, 0])
+        wait(stage_d.at[slot], out_sem.at[slot, 1])
 
     def combine(s, j):
         here = pl.ds(j * HALF, HALF)
@@ -335,11 +329,11 @@
     forward(3, 1, 1)
     sum_cores(2)
     sum_planes(1)
-    weight_grads(0)
     hand_over(3)
     compute(3)
     sum_cores(3)
     sum_planes(2)
+    weight_grads(0)
     weight_grads(1)
     for s in (0, 1):
         combine(s, 0)
@@ -359,17 +353,15 @@
     for dz in (1, 2, 3):
         push(gt_z.at[z], gt_z.at[z], gtz_send.at[dz], gtz_recv.at[dz], along_z(dz))
     weight_grads(3)
-    outs = (
-        (stage_gu.at[:, pl.ds(0, HID)], ggw_o), (stage_gu.at[:, pl.ds(HID, HID)], guw_o), (stage_d, gdw_o),
-    )
-    for i, (src, dst) in enumerate(outs):
-        pltpu.make_async_copy(src, dst, out_sem.at[i]).start()
+    weight_grads(4)
     wait(comb_sib.at[1], cs_recv.at[1])
     opp_out[...] = (comb[1, :, window(c)] + comb_sib[1]).astype(BF16)
     push(opp_out, opp_in, op_send, op_recv, along_z(2))
     combine(0, 2)
+    weight_grads(5)
     combine(0, 3)
     trade(0)
+    weight_grads(6)
 
     for dz in (1, 2, 3):
         wait(gt_z.at[lax.rem(z + 4 - dz, 4)], gtz_recv.at[dz])
@@ -395,8 +387,8 @@
     def _():
         gin_o[...] = result[WIN - QUART // 2:WIN, :]
 
-    for i, (src, dst) in enumerate(outs):
-        pltpu.make_async_copy(src, dst, out_sem.at[i]).wait()
+    for slot in (0, 1):
+        drain(slot)
     wait(send.at[pl.ds(CAP, ROWS - CAP)], disp_send)
     wait(grecv.at[pl.ds(1, 15)], gate_send)
     wait(gt_recv.at[pl.ds(1, 15)], gts_send)
@@ -422,6 +414,36 @@
     for s in (0, 1):
         wait(comb_sib.at[s], cs_send.at[s])
     wait(opp_out, op_send)
+
+
+def widen(gin, gg, ggu, gdw, gin_o, gg_o, ggw_o, guw_o, gdw_o, gu, d, gw, uw, dw, in_sem, out_sem):
+    cuts = [pl.ds(t * TILE, TILE) for t in range(FEAT // TILE)]
+    loads = []
+    for t, cut in enumerate(cuts):
+        pair = (
+            pltpu.make_async_copy(ggu.at[cut], gu.at[cut], in_sem.at[t, 0]),
+            pltpu.make_async_copy(gdw.at[:, cut], d.at[:, cut], in_sem.at[t, 1]),
+        )
+        for copy in pair:
+            copy.start()
+        loads.append(pair)
+    gin_o[...] = gin[...]
+    gg_o[...] = gg[...]
+    stores = []
+    for t, cut in enumerate(cuts):
+        for copy in loads[t]:
+            copy.wait()
+        gw[cut, :] = gu[cut, :HID].astype(F32)
+        uw[cut, :] = gu[cut, HID:].astype(F32)
+        dw[:, cut] = d[:, cut].astype(F32)
+        for i, (src, dst) in enumerate((
+            (gw.at[cut], ggw_o.at[cut]), (uw.at[cut], guw_o.at[cut]), (dw.at[:, cut], gdw_o.at[:, cut]),
+        )):
+            copy = pltpu.make_async_copy(src, dst, out_sem.at[t, i])
+            copy.start()
+            stores.append(copy)
+    for copy in stores:
+        copy.wait()
 
 
 def on_device(saved_input, out_grad, routes, gates, gate_weight, up_weight, down_weight):
@@ -453,10 +475,8 @@
         pltpu.VMEM((2, TOK, WIN), F32),
         pltpu.VMEM((TOK, WIN), BF16),
         pltpu.VMEM((TOK, WIN), BF16),
-        pltpu.VMEM((FEAT, 2 * HID), F32),
-        pltpu.VMEM((HID, FEAT), F32),
-        pltpu.VMEM((FEAT, 2 * HID), BF16),
-        pltpu.VMEM((HID, FEAT), BF16),
+        pltpu.VMEM((2, TILE, 2 * HID), BF16),
+        pltpu.VMEM((2, HID, TILE), BF16),
         dma((3,)),
         dma(()), dma((5, 2)),
         dma(()), dma(()),
@@ -470,27 +490,43 @@
         dma((4,)), dma((4,)),
         dma((2,)), dma((2,)),
         dma(()), dma(()),
-        dma((3,)),
+        dma((2, 2)),
     ]
-    gin, gg, ggw, guw, gdw = pl.pallas_call(
+    partial_outs = pl.pallas_call(
         kernel,
         out_shape=(
             jax.ShapeDtypeStruct((QUART // 2, TOK), BF16),
             jax.ShapeDtypeStruct((2, TOK), F32),
-            jax.ShapeDtypeStruct((FEAT, HID), BF16),
-            jax.ShapeDtypeStruct((FEAT, HID), BF16),
+            jax.ShapeDtypeStruct((FEAT, 2 * HID), BF16),
             jax.ShapeDtypeStruct((HID, FEAT), BF16),
         ),
         in_specs=[anywhere, anywhere, vmem, vmem, anywhere, anywhere, anywhere],
-        out_specs=(vmem, vmem, anywhere, anywhere, anywhere),
+        out_specs=(vmem, vmem, anywhere, anywhere),
         scratch_shapes=scratch,
         compiler_params=pltpu.CompilerParams(
             collective_id=0, has_side_effects=True, vmem_limit_bytes=62 * 2**20
         ),
         cost_estimate=pl.CostEstimate(flops=15 * 10**9, bytes_accessed=20 * 10**6, transcendentals=10**6),
     )(saved_input, out_grad, routes.T, gates.T, gate_weight[0], up_weight[0], down_weight[0])
-    ggw, guw, gdw = (grad.astype(F32)[None] for grad in (ggw, guw, gdw))
-    return gin.T, gg.T, ggw, guw, gdw
+    gin, gg, ggw, guw, gdw = pl.pallas_call(
+        widen,
+        out_shape=(
+            jax.ShapeDtypeStruct((QUART // 2, TOK), BF16),
+            jax.ShapeDtypeStruct((2, TOK), F32),
+            jax.ShapeDtypeStruct((FEAT, HID), F32),
+            jax.ShapeDtypeStruct((FEAT, HID), F32),
+            jax.ShapeDtypeStruct((HID, FEAT), F32),
+        ),
+        in_specs=[vmem, vmem, anywhere, anywhere],
+        out_specs=(vmem, vmem, anywhere, anywhere, anywhere),
+        scratch_shapes=[
+            pltpu.VMEM((FEAT, 2 * HID), BF16), pltpu.VMEM((HID, FEAT), BF16),
+            pltpu.VMEM((FEAT, HID), F32), pltpu.VMEM((FEAT, HID), F32), pltpu.VMEM((HID, FEAT), F32),
+            dma((FEAT // TILE, 2)), dma((FEAT // TILE, 3)),
+        ],
+        compiler_params=pltpu.CompilerParams(vmem_limit_bytes=62 * 2**20),
+    )(*partial_outs)
+    return gin.T, gg.T, ggw[None], guw[None], gdw[None]
 
 
 def solution(mesh):

time: 115 us -> 111 us (0.965)
  other arithmetic: 8.08 us -> 0 us
  Pallas kernels: 104 us -> 110 us
  local copies, waits for them, and re-layouts: 1.28 us -> 0 us
    broadcast_in_dim x2 -> x0, other arithmetic: 8.08 us -> none  [on_device(): ggw, guw, gdw = (grad.astype(F32)[None] for grad in (ggw, guw, gdw))]
    pallas_call x0 -> x1, Pallas kernels: none -> 7.15 us  [on_device(): pl.pallas_call(widen, out_shape=(jax.ShapeDtypeStruct((QUART // 2, TOK),...]
    pallas_call x1, Pallas kernels: 104 us -> 102 us  [on_device(): pl.pallas_call(kernel, out_shape=(jax.ShapeDtypeStruct((QUART // 2, TOK),...]
    unnamed x8 -> x0, local copies, waits for them, and re-layouts: 1.28 us -> none
where the time goes in v3:
time: 111 us; the launch traced here: 110 us
  Pallas kernels  110 us (99%)
    pallas_call x1, Pallas kernels, on_device(): pl.pallas_call(kernel, out_shape=(jax.ShapeDtypeStruct((QUART // 2, TOK),...  102 us
    pallas_call x1, Pallas kernels, on_device(): pl.pallas_call(widen, out_shape=(jax.ShapeDtypeStruct((QUART // 2, TOK),...  7.15 us

profile of v3, /device:TPU:1, one launch (start us, length us, event | category | flops | bytes accessed | tf_op | source)
XLA Modules:
  0.0 110.4 jit_solution(8572709261416346052)
XLA Ops:
  0.6 102.5 %shard_map.110 = (bf16[448,256]{1,0:T(8,128)(2,1)}, f32[2,256]{1,0:T(2,128)}, bf16[3584,512]{1,0:T(8,128)(2,1)}, bf16[256,3584]{1,0:T(8,128)(2,1)}) custom-call(bf16[256,3584]{1,0:T(8,128)(2,1)} %saved.1, bf16[256,3584]{1,0:T(8,128)(2,1)} %ograd.1, s32[2,256]{1,0:T(2,128)} %bitcast.17, bf16[2,256]{1,0:T(2,128)(2,1)} %bitcast.19, bf16[3584,256]{1,0:T(8,128)(2,1)} %bitcast.13, ...), custom_call_target="tpu_custom_call" | custom-call | flops 15000000512 | bytes 20000000 | tf_op jit(solution)/shard_map/pallas_call | solution.py:495
  103.1 7.1 %shard_map.111 = (bf16[448,256]{1,0:T(8,128)(2,1)}, f32[2,256]{1,0:T(2,128)}, f32[3584,256]{1,0:T(8,128)}, f32[3584,256]{1,0:T(8,128)}, f32[256,3584]{1,0:T(8,128)}) custom-call(bf16[448,256]{1,0:T(8,128)(2,1)} %get-tuple-element.14.gin, f32[2,256]{1,0:T(2,128)} %get-tuple-element.15.gg, bf16[3584,512]{1,0:T(8,128)(2,1)} %get-tuple-element.16.ggu, ...), custom_call_target="tpu_custom_call" | custom-call | tf_op jit(solution)/shard_map/pallas_call | solution.py:511

commit v4 on v3

--- a/solution.py
+++ b/solution.py
@@ -175,7 +175,7 @@
 
     def compute(j):
         here = pl.ds(j * CHUNK, CHUNK)
-        slot = j % 2
+        slot = j
         for h, dz in ((0, 0), (1, 1), (2, 3), (3, 2)):
             wait(xy.at[other, here, quarter(dz)], fs_recv.at[j, h])
         lane = lax.broadcasted_iota(jnp.int32, (CAP, 128), 1)
@@ -198,9 +198,6 @@
         grad_pre[here, HID:2 * HID] = (hidden_grad * act).astype(BF16)
         gt_send[:, here] = jnp.broadcast_to(as_row(term), (8, CHUNK))
 
-        if j >= 2:
-            wait(part.at[slot, pl.ds(0, HALF)], sib_send.at[slot])
-            wait(part.at[slot, pl.ds(0, HALF), pl.ds(0, 2 * QUART)], zr_send.at[slot])
         for dz in (1, 3, 2, 0):
             cut = quarter(dz)
             part[slot, :, cut] = dot(grad_pre[here, :], w[cut, :], ((1,), (1,))).astype(BF16)
@@ -216,7 +213,7 @@
                 push(tile, gt_recv.at[j * 4 + i], gts_send, gts_recv, plane(4 - dx, 4 - dy))
 
     def sum_cores(j):
-        slot = j % 2
+        slot = j
         mine, here = rows(c * HALF, HALF), pl.ds(j * HALF, HALF)
         for h, dz in ((0, 1), (1, 3)):
             cut = quarter(dz)
@@ -246,7 +243,7 @@
                 push(src, dst, ret_send, rsem, device)
 
     def sum_planes(j):
-        slot = j % 2
+        slot = j
         mine, here = rows(c * HALF, HALF), pl.ds(j * HALF, HALF)
         cut = quarter(0)
         wait(sib_in.at[here, cut], sib_recv.at[j, 0])
@@ -315,30 +312,29 @@
     dispatch(3, 1, 0)
     sum_cores(0)
     forward(2, 1)
+    dispatch(3, 0, 1)
+    dispatch(3, 1, 1)
     hand_over(1)
     compute(1)
     forward(3, 0, 0)
-    dispatch(3, 0, 1)
+    forward(3, 1, 0)
+    forward(3, 0, 1)
+    forward(3, 1, 1)
+    hand_over(2)
+    compute(2)
     sum_cores(1)
-    forward(3, 1, 0)
-    dispatch(3, 1, 1)
     sum_planes(0)
-    hand_over(2)
-    forward(3, 0, 1)
-    compute(2)
-    forward(3, 1, 1)
+    hand_over(3)
     sum_cores(2)
-    sum_planes(1)
-    hand_over(3)
     compute(3)
     sum_cores(3)
+    sum_planes(1)
+    weight_grads(0)
     sum_planes(2)
-    weight_grads(0)
     weight_grads(1)
-    for s in (0, 1):
-        combine(s, 0)
-        combine(s, 1)
-    combine(1, 2)
+    combine(0, 0)
+    for j in range(3):
+        combine(1, j)
     weight_grads(2)
     wait(gt_recv, gts_recv)
     low = lax.broadcasted_iota(jnp.int32, (8, 128), 1) < CAP
@@ -357,6 +353,7 @@
     wait(comb_sib.at[1], cs_recv.at[1])
     opp_out[...] = (comb[1, :, window(c)] + comb_sib[1]).astype(BF16)
     push(opp_out, opp_in, op_send, op_recv, along_z(2))
+    combine(0, 1)
     combine(0, 2)
     weight_grads(5)
     combine(0, 3)
@@ -394,7 +391,7 @@
     wait(gt_recv.at[pl.ds(1, 15)], gts_send)
     wait(send, fz_send)
     wait(xy.at[c], fs_send)
-    for slot in (0, 1):
+    for slot in range(4):
         wait(part.at[slot, pl.ds(0, HALF)], sib_send.at[slot])
         wait(part.at[slot, pl.ds(0, HALF), pl.ds(0, 2 * QUART)], zr_send.at[slot])
 
@@ -461,7 +458,7 @@
         pltpu.VMEM((HID, FEAT), BF16),
         pltpu.VMEM((ROWS, 2 * HID), BF16),
         pltpu.VMEM((ROWS, HID), BF16),
-        pltpu.VMEM((2, CHUNK, FEAT), BF16),
+        pltpu.VMEM((4, CHUNK, FEAT), BF16),
         pltpu.VMEM((ROWS // 2, FEAT), BF16),
         pltpu.VMEM((2, ROWS // 2, QUART), BF16),
         pltpu.VMEM((2, ROWS // 2, QUART), BF16),
@@ -482,8 +479,8 @@
         dma(()), dma(()),
         dma(()), dma((4, 2)),
         dma(()), dma((4, 4)),
-        dma((2,)), dma((4, 4)),
-        dma((2,)), dma((4, 2)),
+        dma((4,)), dma((4, 4)),
+        dma((4,)), dma((4, 2)),
         dma(()), dma((2, 4)),
         dma(()), dma(()),
         dma(()), dma(()),

time: 111 us -> 104 us (0.937); the launches traced: 110 us -> 102 us
  Pallas kernels: 110 us -> 101 us
    pallas_call x1, Pallas kernels: 102 us -> 93.7 us  [on_device(): pl.pallas_call(kernel, out_shape=(jax.ShapeDtypeStruct((QUART // 2, TOK),...]
where the time goes in v4:
time: 104 us; the launch traced here: 102 us
  Pallas kernels  101 us (97%)
    pallas_call x1, Pallas kernels, on_device(): pl.pallas_call(kernel, out_shape=(jax.ShapeDtypeStruct((QUART // 2, TOK),...  93.7 us
    pallas_call x1, Pallas kernels, on_device(): pl.pallas_call(widen, out_shape=(jax.ShapeDtypeStruct((QUART // 2, TOK),...  7.15 us

profile of v4, /device:TPU:1, one launch (start us, length us, event | category | flops | bytes accessed | tf_op | source)
XLA Modules:
  0.0 101.7 jit_solution(16871332279035193215)
XLA Ops:
  0.6 93.7 %shard_map.110 = (bf16[448,256]{1,0:T(8,128)(2,1)}, f32[2,256]{1,0:T(2,128)}, bf16[3584,512]{1,0:T(8,128)(2,1)}, bf16[256,3584]{1,0:T(8,128)(2,1)}) custom-call(bf16[256,3584]{1,0:T(8,128)(2,1)} %saved.1, bf16[256,3584]{1,0:T(8,128)(2,1)} %ograd.1, s32[2,256]{1,0:T(2,128)} %bitcast.17, bf16[2,256]{1,0:T(2,128)(2,1)} %bitcast.19, bf16[3584,256]{1,0:T(8,128)(2,1)} %bitcast.13, ...), custom_call_target="tpu_custom_call" | custom-call | flops 15000000512 | bytes 20000000 | tf_op jit(solution)/shard_map/pallas_call | solution.py:492
  94.3 7.1 %shard_map.111 = (bf16[448,256]{1,0:T(8,128)(2,1)}, f32[2,256]{1,0:T(2,128)}, f32[3584,256]{1,0:T(8,128)}, f32[3584,256]{1,0:T(8,128)}, f32[256,3584]{1,0:T(8,128)}) custom-call(bf16[448,256]{1,0:T(8,128)(2,1)} %get-tuple-element.14.gin, f32[2,256]{1,0:T(2,128)} %get-tuple-element.15.gg, bf16[3584,512]{1,0:T(8,128)(2,1)} %get-tuple-element.16.ggu, ...), custom_call_target="tpu_custom_call" | custom-call | tf_op jit(solution)/shard_map/pallas_call | solution.py:508
